TPU v7x, 128 devices: a whole 4x4x4 slice. The times are simulated.
128 devices in a mesh: col: 16 (over x, z_hi, core), row: 8 (over y, z_lo).
Axes of the slice: x: 4, y: 4, z: 4 (z_hi: 2, z_lo: 2; z = z_hi * 2 + z_lo), core: 2. Of those that a mesh axis runs over, the one named last changes fastest.
Arguments:
- act_values: bfloat16 [3072, 8192], P('col', 'row'), may hold values from -0.109375 to 0.109375
- act_exps: int32 [3072, 256], P('col', 'row'), may hold values from -2 to 0
- grad_values: bfloat16 [3072, 34816], P('row', 'col'), may hold values from -6 to 6
- grad_exps: int32 [3072, 1088], P('row', 'col'), may hold values from -2 to 0
- weight_values: bfloat16 [8192, 34816], P('row', 'col'), may hold values from -0.03125 to 0.03125
- weight_exps: int32 [8192, 1088], P('row', 'col'), may hold values from -2 to 0
Outputs:
- input_grad: bfloat16 [3072, 8192], P('col', 'row')
- weight_grad: bfloat16 [8192, 34816], P('row', 'col')
All inputs are finite; a program needn't handle non-finite values.
Results may differ from a plain program's by a relative error of at most 0.0034.
Values may be sent and summed in bfloat16 or wider, within the bound.
A program may use at most 128 MiB of HBM per device.

v0:
```python
import jax
import jax.numpy as jnp
from jax import lax
from jax.sharding import PartitionSpec as P


def scale_blocks(values, exponents):
    height, breadth = values.shape
    group = breadth // exponents.shape[1]
    factor = jnp.exp2(exponents.astype(jnp.float32)).astype(values.dtype)
    return (values.reshape(height, breadth // group, group) * factor[:, :, None]).reshape(
        height, breadth
    )


def shards(act_values, act_exps, grad_values, grad_exps, weight_values, weight_exps):
    weights = scale_blocks(weight_values, weight_exps)
    grad_vals, grad_scales = (
        lax.all_gather(grad_values, "row", axis=0, tiled=True),
        lax.all_gather(grad_exps, "row", axis=0, tiled=True),
    )
    grad_rows = scale_blocks(grad_vals, grad_scales)
    grad_block = grad_rows
    input_grad = lax.psum_scatter(
        lax.dot_general(
            grad_block, weights, (((1,), (1,)), ((), ())), preferred_element_type=jnp.float32
        ),
        "col",
        scatter_dimension=0,
        tiled=True,
    ).astype(jnp.bfloat16)
    grad_block = grad_rows
    weight_sum = lax.dot_general(
        scale_blocks(
            lax.all_gather(act_values, "col", axis=0, tiled=True),
            lax.all_gather(act_exps, "col", axis=0, tiled=True),
        ),
        grad_block,
        (((0,), (0,)), ((), ())),
        preferred_element_type=jnp.float32,
    )
    weight_grad = weight_sum.astype(jnp.bfloat16)
    return (input_grad, weight_grad)


def solution(mesh):
    in_specs = (
        P("col", "row"),
        P("col", "row"),
        P("row", "col"),
        P("row", "col"),
        P("row", "col"),
        P("row", "col"),
    )
    out_specs = (P("col", "row"), P("row", "col"))
    return jax.shard_map(shards, mesh=mesh, in_specs=in_specs, out_specs=out_specs, check_vma=False)
```

profile of v0, /device:TPU:48, one launch (start us, length us, event | category | flops | bytes accessed | tf_op | source)
XLA Modules:
  0.0 497.8 jit_solution(15592975554983724956)
XLA Ops:
  7.2 3.8 copy.14
  11.1 0.0 all-gather.6.cloned.1.call-start
  11.1 0.7 all-gather.6.cloned.1.call-update
  11.8 0.0 reduce-scatter.2.cloned.1.call-start
  11.9 6.5 %copy.15 = bf16[1024,2176]{0,1:T(8,128)(2,1)} copy(bf16[1024,2176]{1,0:T(8,128)(2,1)} %param.10) | data formatting | bytes 8912896 | tf_op args[4]
  18.4 0.1 exponential_convert_fusion.2
  18.4 4.7 bitcast_multiply_fusion.2
  23.1 56.4 %all_gather.13 = s32[3072,68]{0,1:T(8,128)S(1)} all-gather(s32[384,68]{0,1:T(8,128)S(1)} %copy-done.2), channel_id=1, replica_groups=mesh['col'=16,'row'=8] {'row'}, dimensions={0}, use_global_device_ids=true | all-gather | bytes 940032 | tf_op jit(solution)/shard_map/all_gather | solution.py:20
  79.6 0.1 exponential_convert_fusion
  79.7 213.7 %all-gather.4.cloned.1.call-done = bf16[3072,2176]{0,1:T(8,128)(2,1)} async-done(((bf16[384,2176]{0,1:T(8,128)(2,1)}), bf16[3072,2176]{0,1:T(8,128)(2,1)}) %all-gather.4.cloned.1.call-update) | async-done | bytes 13369360 | tf_op jit(solution)/shard_map/all_gather | solution.py:19
  293.4 6.5 %bitcast_multiply_fusion = bf16[3072,2176]{0,1:T(8,128)(2,1)S(1)} fusion(bf16[3072,2176]{0,1:T(8,128)(2,1)} %all-gather.4.cloned.1.call-done, bf16[3072,68]{0,1:T(8,128)(2,1)S(1)} %exponential_convert_fusion), kind=kLoop, calls=%fused_computation | loop fusion | flops 6684672 | bytes 27156480 | tf_op jit(solution)/shard_map/mul | solution.py:11
  299.8 4.8 copy-done
  304.6 20.7 %fusion = f32[3072,1024]{1,0:T(8,128)} fusion(bf16[3072,2176]{0,1:T(8,128)(2,1)S(1)} %bitcast_multiply_fusion, bf16[1024,2176]{0,1:T(8,128)(2,1)} %bitcast_multiply_fusion.2), kind=kOutput, calls=%fused_computation.7 | convolution fusion | flops 13690208256 | bytes 30408704 | tf_op jit(solution)/shard_map/dot_general | solution.py:25
  325.4 0.7 copy-done.3
  326.1 23.0 %all-gather = s32[16,192,32]{1,2,0:T(8,128)S(1)} all-gather(s32[1,192,32]{1,2,0:T(8,128)S(1)} %bitcast.13), channel_id=1, replica_groups=mesh['col'=16,'row'=8] {'col'}, dimensions={0}, use_global_device_ids=true | all-gather | bytes 417792 | tf_op jit(solution)/shard_map/all_gather | solution.py:36
  349.0 0.1 exponential_convert_fusion.1
  349.1 0.2 copy.16
  349.3 0.3 reshape.25
  349.6 14.8 %all-gather.6.cloned.1.call-done = bf16[3072,1024]{1,0:T(8,128)(2,1)} async-done(((bf16[192,1024]{1,0:T(8,128)(2,1)}), bf16[3072,1024]{1,0:T(8,128)(2,1)}) %all-gather.6.cloned.1.call-update) | async-done | bytes 6291472 | tf_op jit(solution)/shard_map/all_gather | solution.py:35
  364.3 8.6 %copy.17 = bf16[3072,1024]{0,1:T(8,128)(2,1)} copy(bf16[3072,1024]{1,0:T(8,128)(2,1)} %all-gather.6.cloned.1.call-done) | data formatting | bytes 12582912 | tf_op jit(solution)/shard_map/all_gather | solution.py:35
  373.0 3.3 bitcast_multiply_fusion.1
  376.2 18.9 %convolution_convert_fusion = bf16[1024,2176]{1,0:T(8,128)(2,1)} fusion(bf16[3072,1024]{0,1:T(8,128)(2,1)S(1)} %bitcast_multiply_fusion.1, bf16[3072,2176]{0,1:T(8,128)(2,1)} %copy-done), kind=kOutput, calls=%fused_computation.2 | convolution fusion | flops 13692436480 | bytes 24117248 | tf_op jit(solution)/shard_map/dot_general | solution.py:33
  395.1 94.2 %reduce-scatter.2.cloned.1.call-done = f32[192,1024]{1,0:T(8,128)} async-done(((f32[3072,1024]{1,0:T(8,128)}), f32[192,1024]{1,0:T(8,128)}) %reduce-scatter.2.cloned.1.call-update) | async-done | bytes 786448 | tf_op jit(solution)/shard_map/reduce_scatter | solution.py:24
  489.3 1.9 convert_element_type.28
  (9 shorter events, 0.1 us)
Async XLA Ops:
  7.2 286.2 %all-gather.4.cloned.1.call-start = ((), (), s32[]{:S(2)}) async-start(), calls=%async_computation.1 | async-start | bytes 15040512 | tf_op jit(solution)/shard_map/all_gather | solution.py:19
  11.0 7.3 %copy-start.1 = (s32[1024,68]{0,1:T(8,128)S(1)}, s32[1024,68]{0,1:T(8,128)}, u32[]{:S(2)}) copy-start(s32[1024,68]{0,1:T(8,128)} %param.11) | copy-start | bytes 835588
  11.1 353.3 %all-gather.6.cloned.1.call-start = ((), (), s32[]{:S(2)}) async-start(), calls=%async_computation.3 | async-start | bytes 6684672 | tf_op jit(solution)/shard_map/all_gather | solution.py:35
  11.8 477.5 %reduce-scatter.2.cloned.1.call-start = ((), (), s32[]{:S(2)}) async-start(), calls=%async_computation.2 | async-start | bytes 13369344 | tf_op jit(solution)/shard_map/reduce_scatter | solution.py:24
  18.4 4.8 copy-start.2
  299.8 4.8 copy-start
  325.3 0.8 copy-start.3
Sparse Core Ops, SparseCore 0:
  11.2 282.1 all-gather.3
  295.7 68.5 all-gather.5
  368.7 120.5 reduce-scatter.1
where the time goes:
time: 500 us; the launch traced here: 498 us
  waiting for transfers between devices  323 us (65%)
  blocking collectives  79.4 us (16%)
  matrix products  39.6 us (8%)
  local copies, waits for them, and re-layouts  24.9 us (5%)
  other arithmetic  16.6 us (3%)
  between operations  13.8 us (3%)
    all_gather x1, waiting for transfers between devices, shards(): lax.all_gather(grad_values, 'row', axis=0, tiled=True)  214 us
    reduce_scatter x1, waiting for transfers between devices, shards(): lax.psum_scatter(lax.dot_general(grad_block, weights, (((1,), (1,)), ((),...  94.2 us
    all_gather x1, blocking collectives, shards(): lax.all_gather(grad_exps, 'row', axis=0, tiled=True)  56.4 us
    all_gather x1, blocking collectives, shards(): lax.all_gather(act_exps, 'col', axis=0, tiled=True)  23 us
    dot_general x1, matrix products, shards(): lax.dot_general(grad_block, weights, (((1,), (1,)), ((), ())), preferred_...  20.7 us
    dot_general x1, matrix products, shards(): lax.dot_general(scale_blocks(lax.all_gather(act_values, 'col', axis=0, ti...  18.9 us
    unnamed x10, local copies, waits for them, and re-layouts  15.9 us
    all_gather x1, waiting for transfers between devices, shards(): lax.all_gather(act_values, 'col', axis=0, tiled=True)  14.8 us
  transfers between devices with their start and end apart: 3, of which 3 were waited for; matrix products, arithmetic and copies ran while one was open for 14% of the time, Pallas kernels for 0%

commit v1 on v0

v1 whole, which is shorter than its diff:
```python
import functools

import jax
import jax.numpy as jnp
from jax import lax
from jax.experimental import pallas as pl
from jax.experimental.pallas import tpu as pltpu
from jax.sharding import PartitionSpec as P

MESH = pl.DeviceIdType.MESH
BF16, F32 = jnp.bfloat16, jnp.float32
BLOCK = 32

OWN = [(0, 0, q) for q in range(4)]
UP = OWN + [(0, 1, 0), (0, 1, 2), (-1, 0, 0), (-1, 0, 2), (-1, 1, 0), (-1, 1, 2)]
DOWN = OWN + [(0, 1, 1), (0, 1, 3), (1, 0, 1), (1, 0, 3), (1, 1, 1), (1, 1, 3)]
ACROSS = OWN + [(-1, 0, 1), (-1, 0, 3), (1, 0, 0), (1, 0, 2)]
HALVES = [
    (0, 0, 0), (0, 0, 1),
    (-1, 0, 0), (1, 0, 0), (0, 1, 0),
    (-1, 0, 1), (1, 0, 1), (0, 1, 1),
    (-1, 1, 0), (-1, 1, 1),
    (2, 0, 0), (1, 1, 0),
    (2, 0, 1), (1, 1, 1),
    (2, 1, 0), (2, 1, 1),
]


def factors(exps, spread):
    scale = jnp.exp2(exps.astype(F32)).astype(BF16)
    return jnp.dot(scale, spread, preferred_element_type=F32).astype(BF16)


def spreader(groups):
    shape = (groups, groups * BLOCK)
    hit = lax.broadcasted_iota(jnp.int32, shape, 1) // BLOCK == lax.broadcasted_iota(jnp.int32, shape, 0)
    return jnp.where(hit, 1.0, 0.0).astype(BF16)


def kernel(
    av_hbm, ae_hbm, gv_hbm, ge_hbm, wv_hbm, we_hbm,
    ig_hbm, wg_hbm,
    g, at, w, acc, wout, ps, pr, xs, xr, cs, zs, zr, out, ge, we, ae, a_own, a_pair, spread,
    in_sem, g_send, g_recv, pair_send, pair_recv, at_send, at_recv, mix_send, mix_recv,
    ps_send, ps_recv, xs_send, xr_recv, z_send, z_recv, out_sem, wout_sem,
):
    col, row = lax.axis_index("col"), lax.axis_index("row")
    x, zh, core = col // 4, (col // 2) % 2, col % 2
    y, zl = row // 2, row % 2

    def at_xz(dx, dz):
        return (((x + dx + 4) % 4) * 4 + ((zh + dz) % 2) * 2 + core, row)

    def at_yz(dy, dz):
        return (col, ((y + dy + 4) % 4) * 2 + (zl + dz) % 2)

    mate = (col + 1 - 2 * core, row)
    up, down, across = at_yz(1, 0), at_yz(-1, 0), at_yz(0, 1)
    right, left, far, over = at_xz(1, 0), at_xz(3, 0), at_xz(2, 0), at_xz(0, 1)

    own = 2 * y + zl
    loads = [
        pltpu.make_async_copy(gv_hbm, g.at[own], in_sem.at[0]),
        pltpu.make_async_copy(ge_hbm, ge, in_sem.at[1]),
        pltpu.make_async_copy(av_hbm, a_own, in_sem.at[2]),
        pltpu.make_async_copy(ae_hbm, ae, in_sem.at[3]),
        pltpu.make_async_copy(wv_hbm, w, in_sem.at[4]),
        pltpu.make_async_copy(we_hbm, we, in_sem.at[5]),
    ]
    for load in loads:
        load.start()

    barrier = pltpu.get_barrier_semaphore()
    peers = (up, down, across, right, left, far, over, mate)
    for peer in peers:
        pl.semaphore_signal(barrier, inc=1, device_id=peer, device_id_type=MESH)

    spread[...] = spreader(spread.shape[0])

    def block(dy, dz):
        return 2 * ((y + dy + 4) % 4) + (zl + dz) % 2

    def g_copy(link, unit):
        dy, dz, q = (UP, DOWN, ACROSS)[link][unit]
        piece = g.at[block(dy, dz), :, pl.ds(48 * q, 48)]
        return pltpu.make_async_remote_copy(
            src_ref=piece, dst_ref=piece, send_sem=g_send.at[link, unit], recv_sem=g_recv.at[link, unit],
            device_id=(up, down, across)[link], device_id_type=MESH,
        )

    def links(unit):
        return [k for k in range(3) if unit < len((UP, DOWN, ACROSS)[k])]

    def g_issue(unit):
        for k in links(unit):
            g_copy(k, unit).start()

    def g_arrived(unit):
        for k in links(unit):
            dy, dz, q = (UP, DOWN, ACROSS)[k][unit]
            piece = g.at[block(dy + (-1, 1, 0)[k], dz + (0, 0, 1)[k]), :, pl.ds(48 * q, 48)]
            pltpu.make_async_remote_copy(
                src_ref=piece, dst_ref=piece, send_sem=g_send.at[k, unit], recv_sem=g_recv.at[k, unit],
                device_id=(up, down, across)[k], device_id_type=MESH,
            ).wait_recv()

    loads[0].wait()
    loads[1].wait()
    for q in range(4):
        rows = pl.ds(48 * q, 48)
        scale = factors(ge[:, rows].reshape(96, ge.shape[2]), spread[...])
        g[own, :, rows] = (g[own, :, rows].reshape(scale.shape) * scale).reshape(2, 48, scale.shape[1])
        if q == 0:
            pl.semaphore_wait(barrier, len(peers))
        if q < 2:
            g_issue(q)

    loads[2].wait()
    loads[3].wait()
    groups = ae.shape[1]
    a_own[...] = a_own[...] * factors(ae[...], spread[:groups, : groups * BLOCK])
    half = a_own.shape[1] // 2
    mine = pl.ds(pl.multiple_of(core * half, half), half)
    theirs = pl.ds(pl.multiple_of((1 - core) * half, half), half)
    pair = pltpu.make_async_remote_copy(
        src_ref=a_own.at[:, theirs], dst_ref=a_pair.at[core], send_sem=pair_send, recv_sem=pair_recv,
        device_id=mate, device_id_type=MESH,
    )
    pair.start()
    a_pair[core] = a_own[:, mine]

    loads[4].wait()
    loads[5].wait()

    def scale_weight(i, carry):
        rows = pl.ds(pl.multiple_of(i * 128, 128), 128)
        w[rows] = w[rows] * factors(we[rows], spread[...])
        return carry

    lax.fori_loop(0, w.shape[0] // 128, scale_weight, 0)

    pair.wait()
    at[2 * x + zh, mine] = a_pair[...].reshape(2 * a_pair.shape[1], half).T

    def at_copy(dx, dz, k, device):
        piece = at.at[2 * ((x + dx) % 4) + (zh + dz) % 2, mine]
        return pltpu.make_async_remote_copy(
            src_ref=piece, dst_ref=piece, send_sem=at_send.at[k], recv_sem=at_recv.at[k],
            device_id=device, device_id_type=MESH,
        )

    def mix_copy(dx, dz, to_me=False):
        k = 2 * dx + dz
        piece = at.at[2 * ((x + dx) % 4) + (zh + dz) % 2, theirs if to_me else mine]
        return pltpu.make_async_remote_copy(
            src_ref=piece, dst_ref=piece, send_sem=mix_send.at[k], recv_sem=mix_recv.at[k],
            device_id=mate, device_id_type=MESH,
        )

    at_sent = [at_copy(0, 0, 0, over)] + [at_copy(0, 0, d, at_xz(d, 0)) for d in (1, 3, 2)]
    for copy in at_sent:
        copy.start()
    mixed = [mix_copy(0, 0)]
    mixed[0].start()

    def at_over():
        at_copy(0, 1, 0, over).wait_recv()
        for d in (1, 3, 2):
            at_sent.append(at_copy(0, 1, 3 + d, at_xz(d, 0)))
            at_sent[-1].start()
        mixed.append(mix_copy(0, 1))
        mixed[-1].start()

    def at_line(dz):
        for d in (1, 3, 2):
            at_copy(4 - d, dz, 3 * dz + d, right).wait_recv()
            mixed.append(mix_copy(4 - d, dz))
            mixed[-1].start()

    def at_whole():
        for dx in range(4):
            for dz in range(2):
                mix_copy(dx, dz, True).wait_recv()

    def target(k):
        dy, dz, _ = HALVES[k]
        return (y + dy + 4) % 4, (zl + dz) % 2

    def ps_copy(k):
        slot = k % 4
        return pltpu.make_async_remote_copy(
            src_ref=ps.at[slot, 1 - core], dst_ref=pr.at[slot], send_sem=ps_send.at[slot], recv_sem=ps_recv.at[slot],
            device_id=mate, device_id_type=MESH,
        )

    def xs_copy(k):
        xt, zt = target(k)
        h = HALVES[k][2]
        apart = (x - xt + 4) % 4
        return pltpu.make_async_remote_copy(
            src_ref=xs.at[k % 4], dst_ref=xr.at[zt, (apart + 3) % 4, h], send_sem=xs_send.at[k % 4],
            recv_sem=xr_recv.at[zt, (apart + 3) % 4, h],
            device_id=(xt * 4 + zh * 2 + core, row), device_id_type=MESH,
        )

    def z_copy(h):
        return pltpu.make_async_remote_copy(
            src_ref=zs.at[h], dst_ref=zr.at[h], send_sem=z_send.at[h], recv_sem=z_recv.at[h],
            device_id=over, device_id_type=MESH,
        )

    def compute(k):
        dy, dz, h = HALVES[k]
        if k >= 4:
            ps_copy(k - 4).wait_send()
        b = block(dy, dz)

        def tile(n, carry):
            rows = pl.ds(pl.multiple_of(n * 256, 256), 256)
            part = lax.dot_general(
                g[b, :, pl.ds(96 * h, 96)].reshape(192, g.shape[3]), w[rows], (((1,), (1,)), ((), ())),
                preferred_element_type=F32,
            )
            ps[k % 4, :, :, rows] = part.reshape(2, 96, 256)
            return carry

        lax.fori_loop(0, w.shape[0] // 256, tile, 0)
        ps_copy(k).start()

    def consume(k):
        h = HALVES[k][2]
        xt, zt = target(k)
        ps_copy(k).wait_recv()

        @pl.when(xt == x)
        def _():
            cs[zt, h] = ps[k % 4, core] + pr[k % 4]

        if k >= 4:
            @pl.when(target(k - 4)[0] != x)
            def _():
                xs_copy(k - 4).wait_send()

        @pl.when(xt != x)
        def _():
            xs[k % 4] = (ps[k % 4, core] + pr[k % 4]).astype(BF16)
            xs_copy(k).start()

    def collect(k):
        h = HALVES[k][2]
        xt, zt = target(k)

        @pl.when(xt == x)
        def _():
            for j in range(3):
                pltpu.make_async_remote_copy(
                    src_ref=xs.at[0], dst_ref=xr.at[zt, j, h], send_sem=xs_send.at[0], recv_sem=xr_recv.at[zt, j, h],
                    device_id=right, device_id_type=MESH,
                ).wait_recv()
            total = (cs[zt, h] + xr[zt, 0, h].astype(F32)) + (xr[zt, 1, h].astype(F32) + xr[zt, 2, h].astype(F32))

            @pl.when(zt == zh)
            def _():
                cs[zt, h] = total

            @pl.when(zt != zh)
            def _():
                zs[h] = total.astype(BF16)
                z_copy(h).start()

    def tiles(dy, dz, count, first, last, low, high):
        b = block(dy, dz) if count == 1 else 2 * ((y + dy + 4) % 4)

        def part(cols, size):
            if count == 1:
                lhs = at[b]
            else:
                lhs = jnp.concatenate([at[b], at[b + 1]], axis=1)
            rhs = g[pl.ds(b, count), :, :, cols].reshape(count * 384, size)
            value = jnp.dot(lhs, rhs, preferred_element_type=F32)
            if not first:
                value = acc[:, cols] + value
            if last:
                wout[:, cols] = value.astype(BF16)
            else:
                acc[:, cols] = value

        def tile(n, carry):
            part(pl.ds(pl.multiple_of(n * 256, 256), 256), 256)
            return carry

        full = g.shape[3] // 256
        lax.fori_loop(low, min(high, full), tile, 0)
        if high > full:
            part(pl.ds(full * 256, g.shape[3] - full * 256), g.shape[3] - full * 256)

    def wout_copy(i):
        cols = (pl.ds(0, 1024), pl.ds(1024, 1152))[i]
        return pltpu.make_async_copy(wout.at[:, cols], wg_hbm.at[:, cols], wout_sem.at[i])

    compute(0)
    compute(1)
    consume(0)
    consume(1)
    g_arrived(0)
    g_issue(2)
    at_over()
    g_arrived(1)
    g_issue(3)
    compute(2)
    compute(3)
    consume(2)
    compute(4)
    consume(3)
    at_line(0)
    collect(0)
    collect(1)
    consume(4)
    g_arrived(2)
    g_issue(4)
    g_arrived(3)
    g_issue(5)
    compute(5)
    compute(6)
    consume(5)
    compute(7)
    consume(6)
    collect(2)
    collect(3)
    collect(4)
    consume(7)
    g_arrived(4)
    g_issue(6)
    compute(8)
    at_line(1)
    consume(8)
    g_arrived(5)
    g_issue(7)
    compute(9)
    at_whole()
    consume(9)
    collect(5)
    collect(6)
    collect(7)
    tiles(0, 0, 2, True, False, 0, 9)
    g_arrived(6)
    g_issue(8)
    compute(10)
    compute(11)
    consume(10)
    tiles(-1, 0, 2, False, False, 0, 4)
    consume(11)
    collect(8)
    collect(9)
    tiles(-1, 0, 2, False, False, 4, 9)
    g_arrived(7)
    g_issue(9)
    compute(12)
    compute(13)
    consume(12)
    tiles(1, 0, 2, False, False, 0, 4)
    consume(13)
    collect(10)
    collect(11)
    tiles(1, 0, 2, False, False, 4, 9)
    g_arrived(8)
    compute(14)
    tiles(2, 0, 1, False, False, 0, 4)
    consume(14)
    collect(12)
    collect(13)
    tiles(2, 0, 1, False, False, 4, 9)
    g_arrived(9)
    compute(15)
    tiles(2, 1, 1, False, True, 0, 4)
    consume(15)
    wout_copy(0).start()
    collect(14)
    tiles(2, 1, 1, False, True, 4, 9)
    wout_copy(1).start()
    collect(15)
    for h in range(2):
        z_copy(h).wait_recv()
        out[:, pl.ds(96 * h, 96)] = (cs[zh, h] + zr[h].astype(F32)).astype(BF16).reshape(1, 96, out.shape[2])
    final = pltpu.make_async_copy(out, ig_hbm, out_sem)
    final.start()

    for unit in range(10):
        for k in links(unit):
            g_copy(k, unit).wait_send()
    for copy in at_sent + mixed:
        copy.wait_send()
    for k in range(12, 16):
        ps_copy(k).wait_send()

        @pl.when(target(k)[0] != x)
        def _():
            xs_copy(k).wait_send()

    for h in range(2):
        z_copy(h).wait_send()
    for i in range(2):
        wout_copy(i).wait()
    final.wait()


def shards(act_values, act_exps, grad_values, grad_exps, weight_values, weight_exps):
    tokens, model = act_values.shape
    rows, width = grad_values.shape
    groups = width // BLOCK
    dma = pltpu.SemaphoreType.DMA
    scratch = [
        pltpu.VMEM((8, 2, rows // 2, width), BF16),
        pltpu.VMEM((8, model, rows), BF16),
        pltpu.VMEM((model, width), BF16),
        pltpu.VMEM((model, width), F32),
        pltpu.VMEM((model, width), BF16),
        pltpu.VMEM((4, 2, rows // 4, model), F32),
        pltpu.VMEM((4, rows // 4, model), F32),
        pltpu.VMEM((4, rows // 4, model), BF16),
        pltpu.VMEM((2, 3, 2, rows // 4, model), BF16),
        pltpu.VMEM((2, 2, rows // 4, model), F32),
        pltpu.VMEM((2, rows // 4, model), BF16),
        pltpu.VMEM((2, rows // 4, model), BF16),
        pltpu.VMEM((1, tokens, model), BF16),
        pltpu.VMEM((2, rows // 2, groups), jnp.int32),
        pltpu.VMEM((model, groups), jnp.int32),
        pltpu.VMEM((tokens, model // BLOCK), jnp.int32),
        pltpu.VMEM((tokens, model), BF16),
        pltpu.VMEM((2, tokens, model // 2), BF16),
        pltpu.VMEM((groups, width), BF16),
        dma((6,)),
        dma((3, 10)), dma((3, 10)),
        dma, dma,
        dma((7,)), dma((7,)),
        dma((8,)), dma((8,)),
        dma((4,)), dma((4,)),
        dma((4,)), dma((2, 3, 2)),
        dma((2,)), dma((2,)),
        dma, dma((2,)),
    ]
    anywhere = pl.BlockSpec(memory_space=pl.ANY)
    input_grad, weight_grad = pl.pallas_call(
        kernel,
        out_shape=(
            jax.ShapeDtypeStruct((1, tokens, model), BF16),
            jax.ShapeDtypeStruct((model, width), BF16),
        ),
        in_specs=[anywhere] * 6,
        out_specs=(anywhere, anywhere),
        scratch_shapes=scratch,
        compiler_params=pltpu.CompilerParams(
            collective_id=0, has_side_effects=True, vmem_limit_bytes=60 * 2**20
        ),
        cost_estimate=pl.CostEstimate(
            flops=4 * 8 * rows * model * width, bytes_accessed=16 * 2**20, transcendentals=0
        ),
        name="fused",
    )(
        act_values, act_exps,
        grad_values.reshape(2, rows // 2, width), grad_exps.reshape(2, rows // 2, groups),
        weight_values, weight_exps,
    )
    return input_grad.reshape(tokens, model), weight_grad


def solution(mesh):
    in_specs = (P("col", "row"),) * 2 + (P("row", "col"),) * 4
    out_specs = (P("col", "row"), P("row", "col"))
    return jax.shard_map(shards, mesh=mesh, in_specs=in_specs, out_specs=out_specs, check_vma=False)
```

time: 500 us -> 150 us (0.30)
  waiting for transfers between devices: 323 us -> 0 us
  Pallas kernels: 0 us -> 137 us
  blocking collectives: 79.4 us -> 0 us
  matrix products: 39.6 us -> 0 us
  other arithmetic: 16.6 us -> 0 us
  local copies, waits for them, and re-layouts: 24.9 us -> 11.6 us
  between operations: 13.8 us -> 0.64 us
    all_gather x2 -> x0, waiting for transfers between devices: 228 us -> none  [the longest x1 214 us: shards(): lax.all_gather(grad_values, 'row', axis=0, tiled=True)]
    pallas_call x0 -> x1, Pallas kernels: none -> 137 us  [shards(): pl.pallas_call(kernel, out_shape=(jax.ShapeDtypeStruct((1, tokens, model)...]
    reduce_scatter x1 -> x0, waiting for transfers between devices: 94.2 us -> none  [shards(): lax.psum_scatter(lax.dot_general(grad_block, weights, (((1,), (1,)), ((),...]
    all_gather x2 -> x0, blocking collectives: 79.4 us -> none  [the longest x1 56.4 us: shards(): lax.all_gather(grad_exps, 'row', axis=0, tiled=True)]
    dot_general x2 -> x0, matrix products: 39.6 us -> none  [the longest x1 20.7 us: shards(): lax.dot_general(grad_block, weights, (((1,), (1,)), ((), ())), preferred_...]
    mul x3 -> x0, other arithmetic: 14.4 us -> none  [scale_blocks(): values.reshape(height, breadth // group, group) * factor[:, :, None]]
    all_gather x1 -> x0, local copies, waits for them, and re-layouts: 8.62 us -> none  [shards(): lax.all_gather(act_values, 'col', axis=0, tiled=True)]
    unnamed x10 -> x5, local copies, waits for them, and re-layouts: 15.9 us -> 11.6 us
  transfers between devices with their start and end apart: 3 -> 0, of which waited for: 3 -> 0; matrix products, arithmetic and copies ran while one was open for 14% -> 0% of each run, Pallas kernels for 0% -> 0%
where the time goes in v1:
time: 150 us
  Pallas kernels  137 us (91%)
  local copies, waits for them, and re-layouts  11.6 us (8%)
    pallas_call x1, Pallas kernels, shards(): pl.pallas_call(kernel, out_shape=(jax.ShapeDtypeStruct((1, tokens, model)...  137 us
    unnamed x5, local copies, waits for them, and re-layouts  11.6 us

profile of v1, /device:TPU:48, one launch (start us, length us, event | category | flops | bytes accessed | tf_op | source)
XLA Modules:
  0.0 149.7 jit_solution(6165371500029364964)
XLA Ops:
  0.6 1.5 copy.9.ae_hbm
  2.1 1.7 %copy.8 = s32[384,68]{1,0:T(8,128)} copy(s32[384,68]{0,1:T(8,128)} %param.9) | data formatting | bytes 208896 | tf_op args[3]
  3.8 2.0 %copy.10.we_hbm = s32[1024,68]{1,0:T(8,128)} copy(s32[1024,68]{0,1:T(8,128)} %param.11) | data formatting | bytes 557056 | tf_op args[5]
  5.8 137.5 %fused.1 = (bf16[1,192,1024]{2,1,0:T(8,128)(2,1)}, bf16[1024,2176]{1,0:T(8,128)(2,1)}) custom-call(bf16[192,1024]{1,0:T(8,128)(2,1)} %av_hbm.1, s32[192,32]{1,0:T(8,128)} %copy.9.ae_hbm, bf16[2,192,2176]{2,1,0:T(8,128)(2,1)} %bitcast.5, s32[2,192,68]{2,1,0:T(8,128)} %bitcast.4, bf16[1024,2176]{1,0:T(8,128)(2,1)} %wv_hbm.1, s32[1024,68]{1,0:T(8,128)} %copy.10.we_hbm), custom_call_target="tpu_custom_call" | custom-call | flops 27380416512 | bytes 16777216 | tf_op jit(solution)/shard_map/fused/pallas_call | solution.py:443
  143.3 1.8 %copy.13 = bf16[192,1024]{1,0:T(8,128)(2,1)} copy(bf16[192,1024]{1,0:T(8,128)(2,1)} %bitcast.3) | data formatting | bytes 786432
  145.0 4.7 %copy.14 = bf16[1024,2176]{1,0:T(8,128)(2,1)} copy(bf16[1024,2176]{1,0:T(8,128)(2,1)} %get-tuple-element.9) | data formatting | bytes 8912896

commit v2 on v1

v2 whole, which is shorter than its diff:
```python
import functools

import jax
import jax.numpy as jnp
from jax import lax
from jax.experimental import pallas as pl
from jax.experimental.pallas import tpu as pltpu
from jax.sharding import PartitionSpec as P

MESH = pl.DeviceIdType.MESH
BF16, F32 = jnp.bfloat16, jnp.float32
BLOCK = 32

SIZES = (64, 64, 32, 32)
OFFS = (0, 64, 128, 160)
OWN = [(0, 0, q) for q in range(4)]
UP = OWN + [(0, 1, 1), (-1, 0, 0), (0, 1, 3), (-1, 1, 1), (-1, 0, 2), (-1, 1, 3)]
DOWN = OWN + [(0, 1, 1), (1, 0, 1), (1, 0, 3), (1, 1, 0), (1, 1, 2), (0, 1, 3)]
ACROSS = OWN + [(1, 0, 0), (1, 0, 2), (-1, 0, 0), (-1, 0, 2)]
LINKS = (UP, DOWN, ACROSS)
JOBS = [
    [(0, 0, 0), (0, 0, 1)],
    [(0, 0, 2), (0, 0, 3)],
    [(-1, 0, 0), (-1, 0, 1)],
    [(1, 0, 0), (1, 0, 1)],
    [(-1, 0, 2), (-1, 0, 3), (1, 0, 2), (1, 0, 3)],
    [(0, 1, 0), (0, 1, 1)],
    [(0, 1, 2), (0, 1, 3), (-1, 1, 1)],
    [(2, 0, 0), (2, 0, 1)],
    [(1, 1, 1), (1, 1, 0)],
    [(-1, 1, 3), (2, 0, 3), (1, 1, 2)],
    [(2, 1, 1), (2, 1, 0)],
    [(2, 0, 2), (2, 1, 2), (-1, 1, 0)],
    [(2, 1, 3), (1, 1, 3), (-1, 1, 2)],
]


def factors(exps, spread):
    scale = jnp.exp2(exps.astype(F32)).astype(BF16)
    return lax.dot_general(scale, spread, (((0,), (0,)), ((), ())), preferred_element_type=F32).astype(BF16)


def spreader(groups):
    shape = (groups, groups * BLOCK)
    hit = lax.broadcasted_iota(jnp.int32, shape, 1) // BLOCK == lax.broadcasted_iota(jnp.int32, shape, 0)
    return jnp.where(hit, 1.0, 0.0).astype(BF16)


def kernel(
    av_hbm, ae_hbm, gv_hbm, ge_hbm, wv_hbm, we_hbm,
    out, wout,
    g, at, w, acc, ps, pr, xs, xr, cs, zs, zr, ge, we, ae, a_own, a_pair, spread,
    in_sem, g_send, g_recv, pair_send, pair_recv, at_send, at_recv, mix_send, mix_recv,
    ps_send, ps_recv, xs_send, xr_recv, z_send, z_recv,
):
    col, row = lax.axis_index("col"), lax.axis_index("row")
    x, zh, core = col // 4, (col // 2) % 2, col % 2
    y, zl = row // 2, row % 2

    def at_xz(dx, dz):
        return (((x + dx + 4) % 4) * 4 + ((zh + dz) % 2) * 2 + core, row)

    def at_yz(dy, dz):
        return (col, ((y + dy + 4) % 4) * 2 + (zl + dz) % 2)

    mate = (col + 1 - 2 * core, row)
    up, down, across = at_yz(1, 0), at_yz(-1, 0), at_yz(0, 1)
    right, left, far, over = at_xz(1, 0), at_xz(3, 0), at_xz(2, 0), at_xz(0, 1)

    own = 2 * y + zl
    loads = [
        pltpu.make_async_copy(gv_hbm, g.at[own], in_sem.at[0]),
        pltpu.make_async_copy(ge_hbm, ge, in_sem.at[1]),
        pltpu.make_async_copy(av_hbm, a_own, in_sem.at[2]),
        pltpu.make_async_copy(ae_hbm, ae, in_sem.at[3]),
        pltpu.make_async_copy(wv_hbm, w, in_sem.at[4]),
        pltpu.make_async_copy(we_hbm, we, in_sem.at[5]),
    ]
    for load in loads:
        load.start()

    barrier = pltpu.get_barrier_semaphore()
    peers = (up, down, across, right, left, far, over, mate)
    for peer in peers:
        pl.semaphore_signal(barrier, inc=1, device_id=peer, device_id_type=MESH)

    spread[...] = spreader(spread.shape[0])

    def block(dy, dz):
        return 2 * ((y + dy + 4) % 4) + (zl + dz) % 2

    def rows_of(q):
        return pl.ds(OFFS[q], SIZES[q])

    def g_copy(link, unit, arriving=False):
        dy, dz, q = LINKS[link][unit]
        if arriving:
            dy, dz = dy + (-1, 1, 0)[link], dz + (0, 0, 1)[link]
        piece = g.at[block(dy, dz), :, rows_of(q)]
        return pltpu.make_async_remote_copy(
            src_ref=piece, dst_ref=piece, send_sem=g_send.at[link, unit], recv_sem=g_recv.at[link, unit],
            device_id=(up, down, across)[link], device_id_type=MESH,
        )

    def g_issue(y_unit=None, z_unit=None):
        for link, unit in ((0, y_unit), (1, y_unit), (2, z_unit)):
            if unit is not None:
                g_copy(link, unit).start()

    def g_arrived(y_unit=None, z_unit=None):
        for link, unit in ((0, y_unit), (1, y_unit), (2, z_unit)):
            if unit is not None:
                g_copy(link, unit, True).wait_recv()

    loads[0].wait()
    loads[1].wait()
    scale = factors(ge[...], spread[...])
    g[own] = (g[own].reshape(scale.shape) * scale).reshape(g.shape[1:])
    pl.semaphore_wait(barrier, len(peers))
    g_issue(0, 0)
    g_issue(1, 1)

    loads[2].wait()
    loads[3].wait()
    groups = ae.shape[0]
    a_own[...] = a_own[...] * factors(ae[...], spread[:groups, : groups * BLOCK])
    half = a_own.shape[1] // 2
    mine = pl.ds(pl.multiple_of(core * half, half), half)
    theirs = pl.ds(pl.multiple_of((1 - core) * half, half), half)
    pair = pltpu.make_async_remote_copy(
        src_ref=a_own.at[:, theirs], dst_ref=a_pair.at[core], send_sem=pair_send, recv_sem=pair_recv,
        device_id=mate, device_id_type=MESH,
    )
    pair.start()
    a_pair[core] = a_own[:, mine]

    loads[4].wait()
    loads[5].wait()

    def scale_weight(i, carry):
        rows = pl.ds(pl.multiple_of(i * 128, 128), 128)
        w[rows] = w[rows] * factors(we[:, rows], spread[...])
        return carry

    lax.fori_loop(0, w.shape[0] // 128, scale_weight, 0)

    pair.wait()
    at[2 * x + zh, mine] = a_pair[...].reshape(2 * a_pair.shape[1], half).T

    def at_copy(dx, dz, k, device):
        piece = at.at[2 * ((x + dx) % 4) + (zh + dz) % 2, mine]
        return pltpu.make_async_remote_copy(
            src_ref=piece, dst_ref=piece, send_sem=at_send.at[k], recv_sem=at_recv.at[k],
            device_id=device, device_id_type=MESH,
        )

    def mix_copy(dx, dz, to_me=False):
        k = 2 * dx + dz
        piece = at.at[2 * ((x + dx) % 4) + (zh + dz) % 2, theirs if to_me else mine]
        return pltpu.make_async_remote_copy(
            src_ref=piece, dst_ref=piece, send_sem=mix_send.at[k], recv_sem=mix_recv.at[k],
            device_id=mate, device_id_type=MESH,
        )

    at_sent = [at_copy(0, 0, 0, over)] + [at_copy(0, 0, d, at_xz(d, 0)) for d in (1, 3, 2)]
    for copy in at_sent:
        copy.start()
    mixed = [mix_copy(0, 0)]
    mixed[0].start()

    def at_over():
        at_copy(0, 1, 0, over).wait_recv()
        for d in (1, 3, 2):
            at_sent.append(at_copy(0, 1, 3 + d, at_xz(d, 0)))
            at_sent[-1].start()
        mixed.append(mix_copy(0, 1))
        mixed[-1].start()

    def at_line(dz):
        for d in (1, 3, 2):
            at_copy(4 - d, dz, 3 * dz + d, right).wait_recv()
            mixed.append(mix_copy(4 - d, dz))
            mixed[-1].start()

    def at_whole():
        for dx in range(4):
            for dz in range(2):
                mix_copy(dx, dz, True).wait_recv()

    def target(piece):
        return (y + piece[0] + 4) % 4, (zl + piece[1]) % 2

    def size_of(k):
        return sum(SIZES[piece[2]] for piece in JOBS[k])

    def pieces_of(k):
        start = 0
        for i, piece in enumerate(JOBS[k]):
            yield i, piece, pl.ds(start, SIZES[piece[2]])
            start += SIZES[piece[2]]

    def ps_copy(k):
        slot, rows = k % 4, pl.ds(0, size_of(k))
        return pltpu.make_async_remote_copy(
            src_ref=ps.at[slot, 1 - core, rows], dst_ref=pr.at[slot, rows],
            send_sem=ps_send.at[slot], recv_sem=ps_recv.at[slot], device_id=mate, device_id_type=MESH,
        )

    def xs_copy(k, i, piece, rows):
        xt, zt = target(piece)
        seat, q = (x - xt + 3) % 4, piece[2]
        return pltpu.make_async_remote_copy(
            src_ref=xs.at[k % 4, rows], dst_ref=xr.at[zt, seat, rows_of(q)],
            send_sem=xs_send.at[k % 4, i], recv_sem=xr_recv.at[zt, seat, q],
            device_id=(xt * 4 + zh * 2 + core, row), device_id_type=MESH,
        )

    def z_copy(q):
        return pltpu.make_async_remote_copy(
            src_ref=zs.at[rows_of(q)], dst_ref=zr.at[rows_of(q)], send_sem=z_send.at[q], recv_sem=z_recv.at[q],
            device_id=over, device_id_type=MESH,
        )

    def compute(k):
        if k >= 4:
            ps_copy(k - 4).wait_send()
        total = size_of(k)

        def tile(n, carry):
            cols = pl.ds(pl.multiple_of(n * 256, 256), 256)
            parts = [g[block(dy, dz), :, rows_of(q)] for dy, dz, q in JOBS[k]]
            lhs = jnp.concatenate(parts, axis=1).reshape(2 * total, g.shape[3])
            part = lax.dot_general(lhs, w[cols], (((1,), (1,)), ((), ())), preferred_element_type=F32)
            ps[k % 4, :, pl.ds(0, total), cols] = part.reshape(2, total, 256)
            return carry

        lax.fori_loop(0, w.shape[0] // 256, tile, 0)
        ps_copy(k).start()

    def xs_sent(k):
        for i, piece, rows in pieces_of(k):
            @pl.when(target(piece)[0] != x)
            def _():
                xs_copy(k, i, piece, rows).wait_send()

    def consume(k):
        ps_copy(k).wait_recv()
        if k >= 4:
            xs_sent(k - 4)
        for i, piece, rows in pieces_of(k):
            xt, zt = target(piece)

            @pl.when(xt == x)
            def _():
                cs[zt, rows_of(piece[2])] = ps[k % 4, core, rows] + pr[k % 4, rows]

            @pl.when(xt != x)
            def _():
                xs[k % 4, rows] = (ps[k % 4, core, rows] + pr[k % 4, rows]).astype(BF16)
                xs_copy(k, i, piece, rows).start()

    def collect(k):
        for _, piece, _ in pieces_of(k):
            collect_piece(piece)

    def collect_piece(piece):
        q = piece[2]
        xt, zt = target(piece)
        rows = rows_of(q)

        @pl.when(xt == x)
        def _():
            for j in range(3):
                pltpu.make_async_remote_copy(
                    src_ref=xs.at[0, pl.ds(0, SIZES[q])], dst_ref=xr.at[zt, j, rows], send_sem=xs_send.at[0, 0],
                    recv_sem=xr_recv.at[zt, j, q], device_id=right, device_id_type=MESH,
                ).wait_recv()
            total = (cs[zt, rows] + xr[zt, 0, rows].astype(F32)) + (
                xr[zt, 1, rows].astype(F32) + xr[zt, 2, rows].astype(F32)
            )

            @pl.when(zt == zh)
            def _():
                cs[zt, rows] = total

            @pl.when(zt != zh)
            def _():
                zs[rows] = total.astype(BF16)
                z_copy(q).start()

    def tiles(pairs, first, last, low, high):
        blocks = [block(dy, dz) for dy, dz in pairs]
        depth = len(blocks) * g.shape[1] * g.shape[2]

        def part(cols, size):
            lhs = jnp.concatenate([at[b] for b in blocks], axis=1)
            rhs = jnp.concatenate([g[b, :, :, cols] for b in blocks], axis=0).reshape(depth, size)
            value = jnp.dot(lhs, rhs, preferred_element_type=F32)
            if not first:
                value = acc[:, cols] + value
            if last:
                wout[:, cols] = value.astype(BF16)
            else:
                acc[:, cols] = value

        def tile(n, carry):
            part(pl.ds(pl.multiple_of(n * 256, 256), 256), 256)
            return carry

        full = g.shape[3] // 256
        lax.fori_loop(low, min(high, full), tile, 0)
        if high > full:
            part(pl.ds(full * 256, g.shape[3] - full * 256), g.shape[3] - full * 256)

    compute(0)
    compute(1)
    consume(0)
    consume(1)
    g_arrived(0)
    g_issue(2)
    g_arrived(1, 0)
    g_issue(3, 2)
    compute(2)
    compute(3)
    consume(2)
    consume(3)
    at_over()
    g_arrived(2, 1)
    g_issue(4, 3)
    g_arrived(3, 2)
    g_issue(5, 4)
    compute(4)
    compute(5)
    consume(4)
    at_line(0)
    consume(5)
    collect(0)
    collect(1)
    g_arrived(4, 3)
    g_issue(6, 5)
    compute(6)
    collect(2)
    collect(3)
    consume(6)
    g_arrived(5, 4)
    g_issue(7, 6)
    compute(7)
    compute(8)
    consume(7)
    at_line(1)
    consume(8)
    collect(4)
    collect(5)
    g_arrived(6, 5)
    g_issue(8, 7)
    compute(9)
    at_whole()
    consume(9)
    collect(6)
    tiles([(0, 0), (0, 1)], True, False, 0, 9)
    g_arrived(7)
    g_issue(9)
    compute(10)
    collect(7)
    consume(10)
    tiles([(-1, 0), (1, 0)], False, False, 0, 9)
    g_arrived(8, 6)
    compute(11)
    collect(8)
    collect(9)
    consume(11)
    g_arrived(9, 7)
    compute(12)
    collect(10)
    rest = [(1, 1), (2, 0), (-1, 1), (2, 1)]
    tiles(rest, False, True, 0, 2)
    consume(12)
    tiles(rest, False, True, 2, 5)
    collect(11)
    tiles(rest, False, True, 5, 8)
    collect(12)
    tiles(rest, False, True, 8, 9)
    for q in range(4):
        z_copy(q).wait_recv()
        out[0, rows_of(q)] = (cs[zh, rows_of(q)] + zr[rows_of(q)].astype(F32)).astype(BF16)

    for link, units in enumerate(LINKS):
        for unit in range(len(units)):
            g_copy(link, unit).wait_send()
    for copy in at_sent + mixed:
        copy.wait_send()
    for k in range(len(JOBS) - 4, len(JOBS)):
        ps_copy(k).wait_send()
        xs_sent(k)
    for q in range(4):
        z_copy(q).wait_send()


def shards(act_values, act_exps, grad_values, grad_exps, weight_values, weight_exps):
    tokens, model = act_values.shape
    rows, width = grad_values.shape
    groups = width // BLOCK
    dma = pltpu.SemaphoreType.DMA
    scratch = [
        pltpu.VMEM((8, 2, rows // 2, width), BF16),
        pltpu.VMEM((8, model, rows), BF16),
        pltpu.VMEM((model, width), BF16),
        pltpu.VMEM((model, width), F32),
        pltpu.VMEM((4, 2, 128, model), F32),
        pltpu.VMEM((4, 128, model), F32),
        pltpu.VMEM((4, 128, model), BF16),
        pltpu.VMEM((2, 3, rows // 2, model), BF16),
        pltpu.VMEM((2, rows // 2, model), F32),
        pltpu.VMEM((rows // 2, model), BF16),
        pltpu.VMEM((rows // 2, model), BF16),
        pltpu.VMEM((groups, rows), jnp.int32),
        pltpu.VMEM((groups, model), jnp.int32),
        pltpu.VMEM((model // BLOCK, tokens), jnp.int32),
        pltpu.VMEM((tokens, model), BF16),
        pltpu.VMEM((2, tokens, model // 2), BF16),
        pltpu.VMEM((groups, width), BF16),
        dma((6,)),
        dma((3, 10)), dma((3, 10)),
        dma, dma,
        dma((7,)), dma((7,)),
        dma((8,)), dma((8,)),
        dma((4,)), dma((4,)),
        dma((4, 4)), dma((2, 3, 4)),
        dma((4,)), dma((4,)),
    ]
    anywhere = pl.BlockSpec(memory_space=pl.ANY)
    input_grad, weight_grad = pl.pallas_call(
        kernel,
        out_shape=(pltpu.VMEM((1, tokens, model), BF16), pltpu.VMEM((model, width), BF16)),
        in_specs=[anywhere] * 6,
        out_specs=(pl.BlockSpec(memory_space=pltpu.VMEM),) * 2,
        scratch_shapes=scratch,
        compiler_params=pltpu.CompilerParams(
            collective_id=0, has_side_effects=True, vmem_limit_bytes=56 * 2**20
        ),
        cost_estimate=pl.CostEstimate(
            flops=4 * 8 * rows * model * width, bytes_accessed=16 * 2**20, transcendentals=0
        ),
        name="fused",
    )(
        act_values, act_exps.T,
        grad_values.reshape(2, rows // 2, width), grad_exps.T,
        weight_values, weight_exps.T,
    )
    return input_grad.reshape(tokens, model), weight_grad


def solution(mesh):
    in_specs = (P("col", "row"),) * 2 + (P("row", "col"),) * 4
    out_specs = (P("col", "row"), P("row", "col"))
    return jax.shard_map(shards, mesh=mesh, in_specs=in_specs, out_specs=out_specs, check_vma=False)
```

time: 150 us -> 122 us (0.81); the launches traced: 150 us -> 120 us
  Pallas kernels: 137 us -> 117 us
  local copies, waits for them, and re-layouts: 11.6 us -> 2.85 us
    pallas_call x1, Pallas kernels: 137 us -> 117 us  [shards(): pl.pallas_call(kernel, out_shape=(pltpu.VMEM((1, tokens, model), BF16), p...]
    unnamed x5 -> x2, local copies, waits for them, and re-layouts: 11.6 us -> 2.85 us
where the time goes in v2:
time: 122 us; the launch traced here: 120 us
  Pallas kernels  117 us (96%)
  local copies, waits for them, and re-layouts  2.85 us (2%)
    pallas_call x1, Pallas kernels, shards(): pl.pallas_call(kernel, out_shape=(pltpu.VMEM((1, tokens, model), BF16), p...  117 us
    unnamed x2, local copies, waits for them, and re-layouts  2.85 us

profile of v2, /device:TPU:48, one launch (start us, length us, event | category | flops | bytes accessed | tf_op | source)
XLA Modules:
  0.0 120.0 jit_solution(6481154773523739104)
XLA Ops:
  0.6 116.5 %fused.1 = (bf16[1,192,1024]{2,1,0:T(8,128)(2,1)S(1)}, bf16[1024,2176]{1,0:T(8,128)(2,1)S(1)}) custom-call(bf16[192,1024]{1,0:T(8,128)(2,1)} %av_hbm.1, s32[32,192]{1,0:T(8,128)} %bitcast.9, bf16[2,192,2176]{2,1,0:T(8,128)(2,1)} %bitcast.6, s32[68,384]{1,0:T(8,128)} %bitcast.8, bf16[1024,2176]{1,0:T(8,128)(2,1)} %wv_hbm.1, s32[68,1024]{1,0:T(8,128)} %bitcast.7), custom_call_target="tpu_custom_call" | custom-call | flops 27380416512 | bytes 16777216 | tf_op jit(solution)/shard_map/fused/pallas_call | solution.py:432
  117.2 0.7 copy.10
  117.9 2.1 %copy.11 = bf16[1024,2176]{1,0:T(8,128)(2,1)} copy(bf16[1024,2176]{1,0:T(8,128)(2,1)S(1)} %get-tuple-element.7) | data formatting | bytes 8912896

commit v3 on v2

--- a/solution.py
+++ b/solution.py
@@ -11,27 +11,36 @@
 BF16, F32 = jnp.bfloat16, jnp.float32
 BLOCK = 32
 
-SIZES = (64, 64, 32, 32)
-OFFS = (0, 64, 128, 160)
-OWN = [(0, 0, q) for q in range(4)]
-UP = OWN + [(0, 1, 1), (-1, 0, 0), (0, 1, 3), (-1, 1, 1), (-1, 0, 2), (-1, 1, 3)]
-DOWN = OWN + [(0, 1, 1), (1, 0, 1), (1, 0, 3), (1, 1, 0), (1, 1, 2), (0, 1, 3)]
-ACROSS = OWN + [(1, 0, 0), (1, 0, 2), (-1, 0, 0), (-1, 0, 2)]
+SIZES = (64, 32, 64, 32, 16, 16, 16, 16, 48, 16, 48, 16)
+OFFS = (0, 64, 96, 160, 160, 176, 64, 80, 96, 144, 0, 48)
+UP = [
+    (0, 0, 0), (0, 0, 1), (0, 0, 2), (0, 0, 3), (0, 1, 0), (-1, 0, 0), (-1, 1, 0), (-1, 1, 1), (-1, 0, 1),
+    (0, 1, 4), (0, 1, 5),
+]
+DOWN = [
+    (0, 0, 0), (0, 0, 2), (0, 0, 1), (0, 0, 3), (0, 1, 2), (1, 0, 2), (1, 1, 2), (1, 1, 3), (1, 0, 3),
+    (0, 1, 6), (0, 1, 7),
+]
+ACROSS = [
+    (0, 0, 0), (0, 0, 2), (0, 0, 1), (0, 0, 3), (-1, 0, 1), (1, 0, 3), (1, 0, 10), (-1, 0, 8), (1, 0, 11),
+    (-1, 0, 9),
+]
 LINKS = (UP, DOWN, ACROSS)
 JOBS = [
-    [(0, 0, 0), (0, 0, 1)],
-    [(0, 0, 2), (0, 0, 3)],
-    [(-1, 0, 0), (-1, 0, 1)],
-    [(1, 0, 0), (1, 0, 1)],
-    [(-1, 0, 2), (-1, 0, 3), (1, 0, 2), (1, 0, 3)],
-    [(0, 1, 0), (0, 1, 1)],
-    [(0, 1, 2), (0, 1, 3), (-1, 1, 1)],
-    [(2, 0, 0), (2, 0, 1)],
-    [(1, 1, 1), (1, 1, 0)],
-    [(-1, 1, 3), (2, 0, 3), (1, 1, 2)],
-    [(2, 1, 1), (2, 1, 0)],
-    [(2, 0, 2), (2, 1, 2), (-1, 1, 0)],
-    [(2, 1, 3), (1, 1, 3), (-1, 1, 2)],
+    [(0, 0, 0), (0, 0, 1), (0, 0, 3)],
+    [(0, 0, 2), (-1, 0, 0)],
+    [(1, 0, 0), (1, 0, 2)],
+    [(-1, 0, 1), (-1, 0, 2), (1, 0, 1)],
+    [(0, 1, 0), (0, 1, 2)],
+    [(-1, 0, 3), (1, 0, 3), (0, 1, 1)],
+    [(-1, 1, 0), (1, 1, 2)],
+    [(2, 0, 0), (2, 0, 2)],
+    [(0, 1, 3), (-1, 1, 1), (1, 1, 3)],
+    [(2, 1, 0), (2, 1, 2)],
+    [(2, 1, 1), (2, 1, 3), (1, 1, 10)],
+    [(2, 0, 1), (2, 0, 3), (-1, 1, 8)],
+    [(-1, 1, 4), (1, 1, 6), (1, 1, 11)],
+    [(-1, 1, 5), (1, 1, 7), (-1, 1, 9)],
 ]
 
 
@@ -49,9 +58,9 @@
 def kernel(
     av_hbm, ae_hbm, gv_hbm, ge_hbm, wv_hbm, we_hbm,
     out, wout,
-    g, at, w, acc, ps, pr, xs, xr, cs, zs, zr, ge, we, ae, a_own, a_pair, spread,
+    g, at, w, acc, ps, pr, xs, xr, rr, hs, cs, zs, zr, ge, we, ae, a_own, a_pair, spread,
     in_sem, g_send, g_recv, pair_send, pair_recv, at_send, at_recv, mix_send, mix_recv,
-    ps_send, ps_recv, xs_send, xr_recv, z_send, z_recv,
+    ps_send, ps_recv, xs_send, xr_recv, rr_recv, rs_send, z_send, z_recv,
 ):
     col, row = lax.axis_index("col"), lax.axis_index("row")
     x, zh, core = col // 4, (col // 2) % 2, col % 2
@@ -76,7 +85,7 @@
         pltpu.make_async_copy(wv_hbm, w, in_sem.at[4]),
         pltpu.make_async_copy(we_hbm, we, in_sem.at[5]),
     ]
-    for load in loads:
+    for load in loads[:2]:
         load.start()
 
     barrier = pltpu.get_barrier_semaphore()
@@ -114,10 +123,19 @@
 
     loads[0].wait()
     loads[1].wait()
-    scale = factors(ge[...], spread[...])
-    g[own] = (g[own].reshape(scale.shape) * scale).reshape(g.shape[1:])
-    pl.semaphore_wait(barrier, len(peers))
-    g_issue(0, 0)
+    for load in loads[2:]:
+        load.start()
+    side = g.shape[2]
+    for first in range(0, 2 * side, 128):
+        scale = factors(ge[:, first : first + 128], spread[...])
+        for c in range(2):
+            low, high = max(first, c * side), min(first + 128, (c + 1) * side)
+            if low < high:
+                rows = pl.ds(low - c * side, high - low)
+                g[own, c, rows] = g[own, c, rows] * scale[low - first : high - first]
+        if first == 128:
+            pl.semaphore_wait(barrier, len(peers))
+            g_issue(0, 0)
     g_issue(1, 1)
 
     loads[2].wait()
@@ -196,7 +214,7 @@
     def pieces_of(k):
         start = 0
         for i, piece in enumerate(JOBS[k]):
-            yield i, piece, pl.ds(start, SIZES[piece[2]])
+            yield i, piece, start
             start += SIZES[piece[2]]
 
     def ps_copy(k):
@@ -206,13 +224,57 @@
             send_sem=ps_send.at[slot], recv_sem=ps_recv.at[slot], device_id=mate, device_id_type=MESH,
         )
 
-    def xs_copy(k, i, piece, rows):
+    def place(piece):
         xt, zt = target(piece)
-        seat, q = (x - xt + 3) % 4, piece[2]
-        return pltpu.make_async_remote_copy(
-            src_ref=xs.at[k % 4, rows], dst_ref=xr.at[zt, seat, rows_of(q)],
-            send_sem=xs_send.at[k % 4, i], recv_sem=xr_recv.at[zt, seat, q],
-            device_id=(xt * 4 + zh * 2 + core, row), device_id_type=MESH,
+        apart = (x - xt + 4) % 4
+        return xt, zt, apart, apart // 2
+
+    def relayed(q):
+        return SIZES[q] > 16
+
+    def split(q, half, start):
+        first = (SIZES[q] + 16) // 32 * 16
+        return pl.ds(start + half * first, SIZES[q] - first if half else first)
+
+    def x_peer(there):
+        return (((there + 4) % 4) * 4 + zh * 2 + core, row)
+
+    def rr_copy(k, i, piece, start, side):
+        xt, zt, _, _ = place(piece)
+        q = piece[2]
+        return pltpu.make_async_remote_copy(
+            src_ref=xs.at[k % 4, split(q, side, start)], dst_ref=rr.at[2 * side + zt, split(q, side, OFFS[q])],
+            send_sem=xs_send.at[k % 4, i, side], recv_sem=rr_recv.at[side, zt, q],
+            device_id=x_peer(xt + 1 + 2 * side), device_id_type=MESH,
+        )
+
+    def xs_copy(k, i, piece, start, side):
+        xt, zt, _, _ = place(piece)
+        q = piece[2]
+        return pltpu.make_async_remote_copy(
+            src_ref=xs.at[k % 4, split(q, 1 - side, start)], dst_ref=xr.at[zt, side, split(q, 1 - side, OFFS[q])],
+            send_sem=xs_send.at[k % 4, i, 0], recv_sem=xr_recv.at[zt, side, q, 1 - side],
+            device_id=x_peer(xt), device_id_type=MESH,
+        )
+
+    def xo_copy(k, i, piece, start):
+        xt, zt, apart, _ = place(piece)
+        q = piece[2]
+        seat = (apart + 3) % 4
+        return pltpu.make_async_remote_copy(
+            src_ref=xs.at[k % 4, pl.ds(start, SIZES[q])], dst_ref=xr.at[zt, seat, rows_of(q)],
+            send_sem=xs_send.at[k % 4, i, 0], recv_sem=xr_recv.at[zt, seat, q, 0],
+            device_id=x_peer(xt), device_id_type=MESH,
+        )
+
+    def rs_copy(piece, side):
+        xt, zt, _, _ = place(piece)
+        q = piece[2]
+        rows = split(q, side, OFFS[q])
+        return pltpu.make_async_remote_copy(
+            src_ref=rr.at[2 * side + zt, rows], dst_ref=xr.at[zt, side, rows],
+            send_sem=rs_send.at[side, zt, q], recv_sem=xr_recv.at[zt, side, q, side],
+            device_id=x_peer(xt), device_id_type=MESH,
         )
 
     def z_copy(q):
@@ -226,58 +288,110 @@
             ps_copy(k - 4).wait_send()
         total = size_of(k)
 
-        def tile(n, carry):
-            cols = pl.ds(pl.multiple_of(n * 256, 256), 256)
-            parts = [g[block(dy, dz), :, rows_of(q)] for dy, dz, q in JOBS[k]]
-            lhs = jnp.concatenate(parts, axis=1).reshape(2 * total, g.shape[3])
-            part = lax.dot_general(lhs, w[cols], (((1,), (1,)), ((), ())), preferred_element_type=F32)
-            ps[k % 4, :, pl.ds(0, total), cols] = part.reshape(2, total, 256)
-            return carry
-
-        lax.fori_loop(0, w.shape[0] // 256, tile, 0)
+        parts = [g[block(dy, dz), :, rows_of(q)] for dy, dz, q in JOBS[k]]
+        lhs = jnp.concatenate(parts, axis=1).reshape(2 * total, g.shape[3])
+        part = lax.dot_general(lhs, w[...], (((1,), (1,)), ((), ())), preferred_element_type=F32)
+        ps[k % 4, :, pl.ds(0, total)] = part.reshape(2, total, w.shape[0])
         ps_copy(k).start()
 
     def xs_sent(k):
-        for i, piece, rows in pieces_of(k):
-            @pl.when(target(piece)[0] != x)
+        for i, piece, start in pieces_of(k):
+            apart = place(piece)[2]
+            if not relayed(piece[2]):
+                @pl.when(apart != 0)
+                def _():
+                    xo_copy(k, i, piece, start).wait_send()
+                continue
+
+            @pl.when(apart == 2)
             def _():
-                xs_copy(k, i, piece, rows).wait_send()
+                for side in range(2):
+                    rr_copy(k, i, piece, start, side).wait_send()
+
+            for side in range(2):
+                @pl.when(apart == 1 + 2 * side)
+                def _():
+                    xs_copy(k, i, piece, start, side).wait_send()
 
     def consume(k):
         ps_copy(k).wait_recv()
         if k >= 4:
             xs_sent(k - 4)
-        for i, piece, rows in pieces_of(k):
-            xt, zt = target(piece)
-
-            @pl.when(xt == x)
+        slot = k % 4
+
+        def chip_sum(rows):
+            return ps[slot, core, rows] + pr[slot, rows]
+
+        for i, piece, start in pieces_of(k):
+            _, zt, apart, _ = place(piece)
+            q = piece[2]
+            rows = pl.ds(start, SIZES[q])
+
+            @pl.when(apart == 0)
             def _():
-                cs[zt, rows_of(piece[2])] = ps[k % 4, core, rows] + pr[k % 4, rows]
-
-            @pl.when(xt != x)
+                cs[zt, rows_of(q)] = chip_sum(rows)
+
+            if not relayed(q):
+                @pl.when(apart != 0)
+                def _():
+                    xs[slot, rows] = chip_sum(rows).astype(BF16)
+                    xo_copy(k, i, piece, start).start()
+                continue
+
+            @pl.when(apart == 2)
             def _():
-                xs[k % 4, rows] = (ps[k % 4, core, rows] + pr[k % 4, rows]).astype(BF16)
-                xs_copy(k, i, piece, rows).start()
+                xs[slot, rows] = chip_sum(rows).astype(BF16)
+                for side in range(2):
+                    rr_copy(k, i, piece, start, side).start()
+
+            for side in range(2):
+                @pl.when(apart == 1 + 2 * side)
+                def _():
+                    now = split(q, 1 - side, start)
+                    xs[slot, now] = chip_sum(now).astype(BF16)
+                    xs_copy(k, i, piece, start, side).start()
+                    hs[side, zt, split(q, side, OFFS[q])] = chip_sum(split(q, side, start))
+
+    def relay(k):
+        for piece in JOBS[k]:
+            _, zt, apart, _ = place(piece)
+            q = piece[2]
+            if not relayed(q):
+                continue
+            for side in range(2):
+                @pl.when(apart == 1 + 2 * side)
+                def _():
+                    part = split(q, side, OFFS[q])
+                    pltpu.make_async_remote_copy(
+                        src_ref=rr.at[2 * side + zt, part], dst_ref=rr.at[2 * side + zt, part], send_sem=xs_send.at[0, 0, 0],
+                        recv_sem=rr_recv.at[side, zt, q], device_id=right, device_id_type=MESH,
+                    ).wait_recv()
+                    rr[2 * side + zt, part] = (hs[side, zt, part] + rr[2 * side + zt, part].astype(F32)).astype(BF16)
+                    rs_copy(piece, side).start()
 
     def collect(k):
-        for _, piece, _ in pieces_of(k):
+        for piece in JOBS[k]:
             collect_piece(piece)
 
     def collect_piece(piece):
         q = piece[2]
-        xt, zt = target(piece)
+        _, zt, apart, _ = place(piece)
         rows = rows_of(q)
 
-        @pl.when(xt == x)
+        @pl.when(apart == 0)
         def _():
-            for j in range(3):
+            if relayed(q):
+                parts = [(side, half, split(q, half, OFFS[q])) for side in range(2) for half in range(2)]
+            else:
+                parts = [(seat, 0, rows) for seat in range(3)]
+            for seat, half, part in parts:
                 pltpu.make_async_remote_copy(
-                    src_ref=xs.at[0, pl.ds(0, SIZES[q])], dst_ref=xr.at[zt, j, rows], send_sem=xs_send.at[0, 0],
-                    recv_sem=xr_recv.at[zt, j, q], device_id=right, device_id_type=MESH,
+                    src_ref=xr.at[zt, seat, part], dst_ref=xr.at[zt, seat, part], send_sem=xs_send.at[0, 0, 0],
+                    recv_sem=xr_recv.at[zt, seat, q, half], device_id=right, device_id_type=MESH,
                 ).wait_recv()
-            total = (cs[zt, rows] + xr[zt, 0, rows].astype(F32)) + (
-                xr[zt, 1, rows].astype(F32) + xr[zt, 2, rows].astype(F32)
-            )
+            total = cs[zt, rows] + (xr[zt, 0, rows].astype(F32) + xr[zt, 1, rows].astype(F32))
+            if not relayed(q):
+                total = total + xr[zt, 2, rows].astype(F32)
 
             @pl.when(zt == zh)
             def _():
@@ -287,6 +401,42 @@
             def _():
                 zs[rows] = total.astype(BF16)
                 z_copy(q).start()
+
+    blocks = {}
+    for job in JOBS:
+        for piece in job:
+            blocks.setdefault(piece[:2], []).append(piece)
+
+    def finish():
+        for pieces in blocks.values():
+            xt, zt = target(pieces[0])
+
+            @pl.when((xt == x) & (zt == zh))
+            def _():
+                for piece in pieces:
+                    z_copy(piece[2]).wait_recv()
+                out[0] = (cs[zh] + zr[...].astype(F32)).astype(BF16)
+
+    def blocks_sent():
+        for pieces in blocks.values():
+            xt, zt, apart, _ = place(pieces[0])
+
+            @pl.when((apart == 0) & (zt != zh))
+            def _():
+                for piece in pieces:
+                    z_copy(piece[2]).wait_send()
+
+            for side in range(2):
+                @pl.when(apart == 1 + 2 * side)
+                def _():
+                    for piece in pieces:
+                        if relayed(piece[2]):
+                            rs_copy(piece, side).wait_send()
+
+    def g_sent(low, high):
+        for link, units in enumerate(LINKS):
+            for unit in range(low, min(high, len(units))):
+                g_copy(link, unit).wait_send()
 
     def tiles(pairs, first, last, low, high):
         blocks = [block(dy, dz) for dy, dz in pairs]
@@ -303,97 +453,113 @@
             else:
                 acc[:, cols] = value
 
-        def tile(n, carry):
-            part(pl.ds(pl.multiple_of(n * 256, 256), 256), 256)
-            return carry
-
-        full = g.shape[3] // 256
-        lax.fori_loop(low, min(high, full), tile, 0)
-        if high > full:
-            part(pl.ds(full * 256, g.shape[3] - full * 256), g.shape[3] - full * 256)
+        for n in range(low, high):
+            part(pl.ds(512 * n, 640 if n == 3 else 512), 640 if n == 3 else 512)
 
     compute(0)
+    g_arrived(0)
+    g_issue(2)
     compute(1)
     consume(0)
     consume(1)
-    g_arrived(0)
-    g_issue(2)
     g_arrived(1, 0)
     g_issue(3, 2)
     compute(2)
-    compute(3)
     consume(2)
-    consume(3)
+    relay(0)
     at_over()
     g_arrived(2, 1)
     g_issue(4, 3)
+    compute(3)
+    compute(4)
+    consume(3)
+    relay(1)
+    relay(2)
+    consume(4)
+    at_line(0)
+    collect(0)
     g_arrived(3, 2)
     g_issue(5, 4)
-    compute(4)
+    g_issue(None, 5)
     compute(5)
-    consume(4)
-    at_line(0)
+    relay(3)
+    relay(4)
+    collect(1)
+    collect(2)
     consume(5)
-    collect(0)
-    collect(1)
     g_arrived(4, 3)
-    g_issue(6, 5)
+    g_issue(6, 6)
     compute(6)
-    collect(2)
+    relay(5)
     collect(3)
     consume(6)
+    collect(4)
     g_arrived(5, 4)
-    g_issue(7, 6)
+    g_arrived(None, 5)
+    g_issue(7, 7)
     compute(7)
+    at_line(1)
+    relay(6)
     compute(8)
     consume(7)
-    at_line(1)
+    collect(5)
     consume(8)
-    collect(4)
-    collect(5)
-    g_arrived(6, 5)
-    g_issue(8, 7)
+    at_whole()
+    near = [(0, 0), (0, 1), (-1, 0), (1, 0)]
+    tiles(near, True, False, 0, 2)
+    g_arrived(6)
+    g_issue(8)
     compute(9)
-    at_whole()
+    relay(7)
+    relay(8)
+    collect(6)
     consume(9)
-    collect(6)
-    tiles([(0, 0), (0, 1)], True, False, 0, 9)
-    g_arrived(7)
-    g_issue(9)
+    tiles(near, True, False, 2, 3)
+    g_arrived(7, 6)
+    g_issue(9, 8)
+    g_issue(None, 9)
     compute(10)
+    relay(9)
     collect(7)
+    collect(8)
     consume(10)
-    tiles([(-1, 0), (1, 0)], False, False, 0, 9)
-    g_arrived(8, 6)
+    tiles(near, True, False, 3, 4)
+    g_sent(0, 7)
+    for copy in at_sent + mixed:
+        copy.wait_send()
+    g_arrived(8, 7)
+    g_issue(10)
     compute(11)
-    collect(8)
+    relay(10)
     collect(9)
     consume(11)
-    g_arrived(9, 7)
+    tiles([(2, 0), (2, 1)], False, False, 0, 1)
+    g_arrived(9, 8)
     compute(12)
+    relay(11)
     collect(10)
-    rest = [(1, 1), (2, 0), (-1, 1), (2, 1)]
-    tiles(rest, False, True, 0, 2)
     consume(12)
-    tiles(rest, False, True, 2, 5)
+    tiles([(2, 0), (2, 1)], False, False, 1, 2)
+    g_arrived(10, 9)
+    compute(13)
+    tiles([(2, 0), (2, 1)], False, False, 2, 3)
+    consume(13)
     collect(11)
-    tiles(rest, False, True, 5, 8)
+    tiles([(2, 0), (2, 1)], False, False, 3, 4)
+    rest = [(-1, 1), (1, 1)]
+    tiles(rest, False, True, 0, 1)
     collect(12)
-    tiles(rest, False, True, 8, 9)
-    for q in range(4):
-        z_copy(q).wait_recv()
-        out[0, rows_of(q)] = (cs[zh, rows_of(q)] + zr[rows_of(q)].astype(F32)).astype(BF16)
-
-    for link, units in enumerate(LINKS):
-        for unit in range(len(units)):
-            g_copy(link, unit).wait_send()
-    for copy in at_sent + mixed:
-        copy.wait_send()
+    tiles(rest, False, True, 1, 2)
+    collect(13)
+    tiles(rest, False, True, 2, 3)
+    tiles(rest, False, True, 3, 4)
+    finish()
+
+    g_sent(7, 11)
     for k in range(len(JOBS) - 4, len(JOBS)):
         ps_copy(k).wait_send()
         xs_sent(k)
-    for q in range(4):
-        z_copy(q).wait_send()
+    blocks_sent()
 
 
 def shards(act_values, act_exps, grad_values, grad_exps, weight_values, weight_exps):
@@ -410,6 +576,8 @@
         pltpu.VMEM((4, 128, model), F32),
         pltpu.VMEM((4, 128, model), BF16),
         pltpu.VMEM((2, 3, rows // 2, model), BF16),
+        pltpu.VMEM((4, rows // 2, model), BF16),
+        pltpu.VMEM((2, 2, rows // 2, model), F32),
         pltpu.VMEM((2, rows // 2, model), F32),
         pltpu.VMEM((rows // 2, model), BF16),
         pltpu.VMEM((rows // 2, model), BF16),
@@ -420,13 +588,14 @@
         pltpu.VMEM((2, tokens, model // 2), BF16),
         pltpu.VMEM((groups, width), BF16),
         dma((6,)),
-        dma((3, 10)), dma((3, 10)),
+        dma((3, 11)), dma((3, 11)),
         dma, dma,
         dma((7,)), dma((7,)),
         dma((8,)), dma((8,)),
         dma((4,)), dma((4,)),
-        dma((4, 4)), dma((2, 3, 4)),
-        dma((4,)), dma((4,)),
+        dma((4, 3, 2)), dma((2, 3, 12, 2)),
+        dma((2, 2, 12)), dma((2, 2, 12)),
+        dma((12,)), dma((12,)),
     ]
     anywhere = pl.BlockSpec(memory_space=pl.ANY)
     input_grad, weight_grad = pl.pallas_call(
@@ -436,7 +605,7 @@
         out_specs=(pl.BlockSpec(memory_space=pltpu.VMEM),) * 2,
         scratch_shapes=scratch,
         compiler_params=pltpu.CompilerParams(
-            collective_id=0, has_side_effects=True, vmem_limit_bytes=56 * 2**20
+            collective_id=0, has_side_effects=True, vmem_limit_bytes=58 * 2**20
         ),
         cost_estimate=pl.CostEstimate(
             flops=4 * 8 * rows * model * width, bytes_accessed=16 * 2**20, transcendentals=0

time: 122 us -> 120 us (0.984)
  the two profiles are of different devices: /device:TPU:48 before, /device:TPU:8 now
where the time goes in v3:
time: 120 us
  Pallas kernels  116 us (97%)
  local copies, waits for them, and re-layouts  2.85 us (2%)
    pallas_call x1, Pallas kernels, shards(): pl.pallas_call(kernel, out_shape=(pltpu.VMEM((1, tokens, model), BF16), p...  116 us
    unnamed x2, local copies, waits for them, and re-layouts  2.85 us

profile of v3, /device:TPU:8, one launch (start us, length us, event | category | flops | bytes accessed | tf_op | source)
XLA Modules:
  0.0 119.9 jit_solution(8934384474288798073)
XLA Ops:
  0.6 116.4 %fused.1 = (bf16[1,192,1024]{2,1,0:T(8,128)(2,1)S(1)}, bf16[1024,2176]{1,0:T(8,128)(2,1)S(1)}) custom-call(bf16[192,1024]{1,0:T(8,128)(2,1)} %av_hbm.1, s32[32,192]{1,0:T(8,128)} %bitcast.9, bf16[2,192,2176]{2,1,0:T(8,128)(2,1)} %bitcast.6, s32[68,384]{1,0:T(8,128)} %bitcast.8, bf16[1024,2176]{1,0:T(8,128)(2,1)} %wv_hbm.1, s32[68,1024]{1,0:T(8,128)} %bitcast.7), custom_call_target="tpu_custom_call" | custom-call | flops 27380416512 | bytes 16777216 | tf_op jit(solution)/shard_map/fused/pallas_call | solution.py:601
  117.1 0.7 copy.10
  117.8 2.1 %copy.11 = bf16[1024,2176]{1,0:T(8,128)(2,1)} copy(bf16[1024,2176]{1,0:T(8,128)(2,1)S(1)} %get-tuple-element.7) | data formatting | bytes 8912896
